TPU v7x, 32 devices: a whole 2x2x4 slice. The times are simulated.
32 devices in a mesh: pulse: 32 (over z, y, x, core), chan: 1.
Axes of the slice: x: 2, y: 2, z: 4, core: 2. Of those that a mesh axis runs over, the one named last changes fastest.
Arguments:
- echoes: bfloat16 [4, 128, 2, 5120], P('chan', 'pulse'), may hold values from -6 to 6
- replica: bfloat16 [2, 4096], replicated, may hold values from -0.0625 to 0.0625
- recon_filters: bfloat16 [4, 4, 2, 64], replicated, may hold values from -0.25 to 0.25
- span_offset: int32 [256], P('pulse'), may hold values from 0 to 4
- span_width: int32 [256], P('pulse'), may hold values from 1 to 4
- aperture_edges: int32 [2, 256], P(None, 'pulse'), may hold values from 0 to 16
Outputs:
- image: bfloat16 [4, 2, 256, 128], P(None, None, 'pulse', 'chan')
All inputs are finite; a program needn't handle non-finite values.
Results may differ from a plain program's by a relative error of at most 0.012.
Values may be sent and summed in bfloat16 or wider, within the bound.
A program may use at most 64 MiB of HBM per device.

v0:
```python
import math

import jax
import jax.numpy as jnp
from jax import lax
from jax.sharding import PartitionSpec as P

MIG = 4
WMAX = 4


def passed_along(array, axis, by):
    count = lax.axis_size(axis)
    pairs = [(i, i + by) for i in range(count) if 0 <= i + by < count]
    return lax.ppermute(array, axis, pairs)


def padded_2(cells, sides, width):
    for axis, dim in sides:
        count = lax.axis_size(axis)
        ends = count - 1
        head = lax.slice_in_dim(cells, 0, width, axis=dim)
        tail = lax.slice_in_dim(cells, cells.shape[dim] - width, cells.shape[dim], axis=dim)
        cells = jnp.concatenate(
            [
                lax.ppermute(tail, axis, [(i, (i + 1) % count) for i in range(ends)]),
                cells,
                lax.ppermute(head, axis, [((i + 1) % count, i) for i in range(ends)]),
            ],
            axis=dim,
        )
    return cells


def banded(taps_row, block_len, span_len):
    period = span_len + 4
    extended = jnp.concatenate([taps_row, jnp.zeros((period - taps_row.shape[0],), taps_row.dtype)])
    tiled = jnp.tile(extended, block_len)[: block_len * span_len]
    return tiled.reshape(block_len, span_len).T


def range_matrix(replica, block_len):
    tap_count = replica.shape[1]
    span_len = 4 * block_len + tap_count
    real_part = banded(replica[0], block_len, span_len)
    imag_part = banded(replica[1], block_len, span_len)
    from_real = jnp.stack([real_part, imag_part], 1)
    from_imag = jnp.stack([-imag_part, real_part], 1)
    matrix = jnp.stack([from_real, from_imag], 0)
    return matrix.reshape(2 * span_len, 2 * block_len)


def compress(echoes, replica):
    channels, pulses, _, samples = echoes.shape
    tap_count = replica.shape[1]
    bin_count = (samples - tap_count) // 4
    block_len = min(128, bin_count)
    span_len = 4 * block_len + tap_count
    block_total = bin_count // block_len
    group = math.gcd(block_total, 8)
    matrix = lax.optimization_barrier(range_matrix(replica, block_len))

    def one_group(group_id):
        windows = [
            lax.dynamic_slice_in_dim(
                echoes, (group_id * group + member) * 4 * block_len, span_len, 3
            )
            for member in range(group)
        ]
        window_rows = jnp.stack(windows, 0).reshape(group * channels * pulses, 2 * span_len)
        return jnp.dot(window_rows, matrix, preferred_element_type=jnp.float32).astype(jnp.bfloat16)

    blocks = lax.map(one_group, jnp.arange(block_total // group, dtype=jnp.int32))
    blocks = blocks.reshape(block_total, channels, pulses, 2, block_len)
    return blocks.transpose(1, 3, 0, 4, 2).reshape(channels, 2, bin_count, pulses)


def migrate(joined, span_offset, span_width):
    bin_count = span_offset.shape[0]
    columns = jnp.arange(joined.shape[2])
    span_first = jnp.arange(bin_count) + span_offset
    within = (columns[None, :] >= span_first[:, None]) & (
        columns[None, :] < (span_first + span_width)[:, None]
    )
    weight = within.astype(jnp.float32) / span_width[:, None].astype(jnp.float32)
    return jnp.einsum(
        "rs,cisp->cirp", weight, joined.astype(jnp.float32), precision=lax.Precision.HIGHEST
    )


def aperture(aperture_edges, pulse_first, pulse_count, all_pulses):
    global_pulse = pulse_first + jnp.arange(pulse_count)
    lower_edge = aperture_edges[0][:, None]
    upper_edge = aperture_edges[1][:, None]
    return (
        (global_pulse[None, :] >= lower_edge) & (global_pulse[None, :] < all_pulses - upper_edge)
    ).astype(jnp.float32)


def azimuth(padded, filters):
    channels, _, bin_count, padded_len = padded.shape
    subbands = filters.shape[0]
    tap_count = filters.shape[3]
    pulses = padded_len - tap_count
    span_len = tap_count + 4
    step_count = span_len // 4
    quartets = padded.reshape(channels, 2, bin_count, padded_len // 4, 4)
    window = jnp.stack(
        [
            quartets[:, :, :, shift_step : shift_step + pulses // 4, :]
            for shift_step in range(step_count)
        ],
        4,
    )
    window = window.transpose(2, 3, 0, 1, 4, 5).reshape(
        bin_count * (pulses // 4), channels * 2 * span_len
    )
    offset = jnp.arange(span_len)[:, None] - jnp.arange(4)[None, :]
    inside = (offset >= 0) & (offset < tap_count)
    tap_index = jnp.clip(offset, 0, tap_count - 1)
    picked = jnp.where(inside, jnp.take(filters, tap_index, axis=3), 0)
    real_part = picked[:, :, 0]
    imag_part = picked[:, :, 1]
    from_real = jnp.stack([real_part, imag_part], 3)
    from_imag = jnp.stack([-imag_part, real_part], 3)
    matrix = jnp.stack([from_real, from_imag], 2)
    matrix = matrix.transpose(1, 2, 3, 0, 4, 5).reshape(channels * 2 * span_len, subbands * 8)
    result = jnp.dot(window, matrix, preferred_element_type=jnp.float32)
    result = result.reshape(bin_count, pulses // 4, subbands, 2, 4).transpose(2, 3, 0, 1, 4)
    return result.reshape(subbands, 2, bin_count, pulses)


def body(echoes, replica, recon_filters, span_offset, span_width, aperture_edges):
    rim_len = MIG + WMAX - 1
    compressed = compress(echoes, replica)
    turned = lax.all_to_all(
        lax.all_to_all(compressed, "pulse", split_axis=2, concat_axis=3, tiled=True),
        "chan",
        split_axis=3,
        concat_axis=0,
        tiled=True,
    )
    pulse_first = lax.axis_index("chan") * turned.shape[3]
    all_pulses = turned.shape[3] * lax.axis_size("chan")
    rim_bins = passed_along(turned[:, :, :rim_len, :], "pulse", -1)
    joined = jnp.concatenate([turned, rim_bins], 2)
    migrated = migrate(joined, span_offset, span_width)
    keep_mask = aperture(aperture_edges, pulse_first, migrated.shape[3], all_pulses)
    corrected = (migrated * keep_mask[None, None]).astype(jnp.bfloat16)
    half_taps = recon_filters.shape[3] // 2
    padded = padded_2(corrected, (("chan", 3),), half_taps)
    image = azimuth(padded, recon_filters)
    return image.astype(jnp.bfloat16)


def solution(mesh):
    return jax.shard_map(
        body,
        mesh=mesh,
        in_specs=(
            P("chan", "pulse", None, None),
            P(),
            P(),
            P("pulse"),
            P("pulse"),
            P(None, "pulse"),
        ),
        out_specs=P(None, None, "pulse", "chan"),
        check_vma=False,
    )
```

profile of v0, /device:TPU:7, one launch (start us, length us, event | category | flops | bytes accessed | tf_op | source)
XLA Modules:
  0.0 122.3 jit_solution(5418667208696302772)
XLA Ops:
  0.0 0.9 slice_reduce_fusion
  1.0 2.1 %tile.21 = bf16[590336]{0:T(1024)(128)(2,1)S(1)} reshape(bf16[128,4612]{1,0:T(8,128)(2,1)S(1)} %tile.20) | data formatting | bytes 2361344 | tf_op jit(solution)/shard_map/tile | solution.py:38
  3.2 1.3 %reshape.147 = bf16[128,4608]{1,0:T(8,128)(2,1)S(1)} reshape(bf16[589824]{0:T(1024)(128)(2,1)S(1)} %slice.117) | data formatting | bytes 2359296 | tf_op jit(solution)/shard_map/reshape | solution.py:39
  4.5 0.7 copy.79
  5.3 1.2 fusion
  6.5 3.1 %tile.9 = bf16[590336]{0:T(1024)(128)(2,1)} reshape(bf16[128,4612]{1,0:T(8,128)(2,1)S(1)} %tile.8) | data formatting | bytes 2361344 | tf_op jit(solution)/shard_map/tile | solution.py:38
  9.6 1.3 %slice-done = bf16[589824]{0:T(1024)(128)(2,1)S(1)} async-done(((bf16[590336]{0:T(1024)(128)(2,1)}), bf16[589824]{0:T(1024)(128)(2,1)S(1)}, s32[]{:S(2)}) %slice-start) | async-done | bytes 1179672 | tf_op jit(solution)/shard_map/slice | solution.py:38
  10.9 1.3 %reshape.146 = bf16[128,4608]{1,0:T(8,128)(2,1)S(1)} reshape(bf16[589824]{0:T(1024)(128)(2,1)S(1)} %slice-done) | data formatting | bytes 2359296 | tf_op jit(solution)/shard_map/reshape | solution.py:39
  12.3 1.4 %copy.78 = bf16[4608,128]{1,0:T(8,128)(2,1)} copy(bf16[4608,128]{0,1:T(8,128)(2,1)S(1)} %bitcast.126) | data formatting | bytes 2359296 | tf_op jit(solution)/shard_map/transpose | solution.py:39
  13.7 2.0 %maximum_bitcast_fusion = (bf16[1,4608,2,128]{3,1,2,0:T(8,128)(2,1)S(1)}, bf16[1,4608,2,128]{3,1,2,0:T(8,128)(2,1)S(1)}) fusion(bf16[4608,1,128]{2,0,1:T(8,128)(2,1)S(1)} %bitcast.125, bf16[4608,1,128]{2,0,1:T(8,128)(2,1)} %bitcast.127, bf16[4608,1,128]{2,0,1:T(8,128)(2,1)S(1)} %copy-done), kind=kLoop, calls=%fused_computation.3 | loop fusion | flops 2359296 | bytes 8257536 | tf_op jit(solution)/shard_map/stack | solution.py:49
  16.1 44.9 %copy.80 = bf16[2,4608,2,128]{3,2,1,0:T(2,128)(2,1)S(1)} copy(bf16[2,4608,2,128]{3,1,2,0:T(8,128)(2,1)S(1)} %pad_maximum_fusion) | data formatting | bytes 9437184 | tf_op jit(solution)/shard_map/stack | solution.py:49
  61.0 2.5 %copy.131 = bf16[1152,8,2,128]{3,1,2,0:T(8,128)(2,1)S(1)} copy(bf16[1152,8,2,128]{3,2,1,0:T(2,128)(2,1)S(1)} %bitcast.124) | data formatting | bytes 9437184
  63.9 0.8 pad_maximum_fusion.1
  64.8 0.9 convolution_convert_fusion.1
  66.3 1.4 %reshape.168 = bf16[32,2,128]{2,1,0:T(2,128)(2,1)} reshape(bf16[256,4,2,4]{3,2,1,0:T(2,128)(2,1)S(1)} %bitcast.131) | data formatting | bytes 32768
  67.7 6.4 %all-to-all-start = ((bf16[32,2,128]{2,1,0:T(2,128)(2,1)}), bf16[32,2,128]{2,1,0:T(2,128)(2,1)S(1)}, u32[]{:S(2)}, u32[]{:S(2)}) async-start(bf16[32,2,128]{2,1,0:T(2,128)(2,1)} %reshape.168), calls=%async_computation | async-start | bytes 32768 | tf_op jit(solution)/shard_map/all_to_all | solution.py:137
  74.4 2.6 %gather_fusion = bf16[272,4,4,2]{2,1,3,0:T(4,128)(2,1)S(1)} fusion(bf16[4,4,2,64]{1,0,3,2:T(4,128)(2,1)S(1)} %copy.107, s32[1024]{0:T(1024)S(1)} %pad_clamp_fusion), kind=kCustom, calls=%fused_computation | custom fusion | bytes 35904 | tf_op jit(solution)/shard_map/jit(_take)/gather | solution.py:121
  77.0 4.0 %copy.124 = bf16[68,4,4,4,2]{1,0,4,3,2:T(8,128)(2,1)S(1)} copy(bf16[68,4,4,4,2]{3,2,4,1,0:T(4,128)(2,1)S(1)} %bitcast.128) | data formatting | bytes 34816 | tf_op jit(solution)/shard_map/jit(_take)/gather | solution.py:121
  82.7 1.1 reshape.169
  83.9 2.2 %copy.121 = bf16[4,2,32,8,4]{3,2,4,1,0:T(8,128)(2,1)S(1)} copy(bf16[4,2,32,8,4]{4,1,0,3,2:T(2,128)(2,1)S(1)} %bitcast.132) | data formatting | bytes 32768 | tf_op jit(solution)/shard_map/all_to_all | solution.py:137
  86.3 2.3 %collective-permute-start = (bf16[4,2,7,128]{3,2,1,0:T(8,128)(2,1)S(1)}, bf16[4,2,7,128]{3,2,1,0:T(8,128)(2,1)S(1)}, u32[]{:S(2)}, u32[]{:S(2)}) collective-permute-start(bf16[4,2,7,128]{3,2,1,0:T(8,128)(2,1)S(1)} %bitcast.138), channel_id=1, source_target_pairs={{1,0},{2,1},{3,2},{4,3},{5,4},{6,5},{7,6},{8,7},{9,8},{10,9},{11,1... | collective-permute-start | bytes 43016 | tf_op jit(solution)/shard_map/ppermute | solution.py:15
  88.7 4.5 %collective-permute-done = bf16[4,2,7,128]{3,2,1,0:T(8,128)(2,1)S(1)} collective-permute-done((bf16[4,2,7,128]{3,2,1,0:T(8,128)(2,1)S(1)}, bf16[4,2,7,128]{3,2,1,0:T(8,128)(2,1)S(1)}, u32[]{:S(2)}, u32[]{:S(2)}) %collective-permute-start) | collective-permute-done | bytes 14368 | tf_op jit(solution)/shard_map/ppermute | solution.py:15
  96.0 3.0 %slice_bitcast_fusion.4 = (bf16[4,2,8,32,1,4]{2,5,3,1,0,4:T(4,128)(2,1)S(1)}, bf16[4,2,8,32,1,4]{2,5,3,1,0,4:T(4,128)(2,1)S(1)}, bf16[4,2,8,32,1,4]{2,5,3,1,0,4:...) fusion(bf16[4,2,8,48,4]{2,4,3,1,0:T(4,128)(2,1)S(1)} %bitcast.122), kind=kLoop, calls=%fused_computation.20 | loop fusion | bytes 557056 | tf_op jit(solution)/shard_map/stack | solution.py:108
  99.0 1.1 copy.88
  100.8 1.7 %copy.89 = bf16[4,2,8,32,1,4]{3,2,5,4,1,0:T(8,128)(2,1)} copy(bf16[4,2,8,32,1,4]{2,5,3,1,0,4:T(4,128)(2,1)} %get-tuple-element.38) | data formatting | bytes 32768 | tf_op jit(solution)/shard_map/stack | solution.py:108
  102.5 1.7 %copy.90 = bf16[4,2,8,32,1,4]{3,2,5,4,1,0:T(8,128)(2,1)} copy(bf16[4,2,8,32,1,4]{2,5,3,1,0,4:T(4,128)(2,1)} %get-tuple-element.37) | data formatting | bytes 32768 | tf_op jit(solution)/shard_map/stack | solution.py:108
  104.2 1.7 %copy.91 = bf16[4,2,8,32,1,4]{3,2,5,4,1,0:T(8,128)(2,1)} copy(bf16[4,2,8,32,1,4]{2,5,3,1,0,4:T(4,128)(2,1)} %get-tuple-element.36) | data formatting | bytes 32768 | tf_op jit(solution)/shard_map/stack | solution.py:108
  105.9 0.8 copy.92
  106.7 0.8 copy.93
  112.6 0.7 constant_dynamic-update-slice_fusion.10
  119.7 1.6 %fusion.1 = bf16[4,2,8,32,4]{3,4,1,0,2:T(4,128)(2,1)S(1)} fusion(bf16[4,2,4,544,1]{3,2,1,0,4:T(4,128)(2,1)S(1)} %copy-done.8, bf16[8,32,544,1,1]{1,0,2,4,3:T(8,128)(2,1)} %bitcast.139), kind=kOutput, calls=%fused_computation.8 | convolution fusion | flops 8921088 | bytes 329728 | tf_op jit(solution)/shard_map/dot_general | solution.py:128
  121.5 0.7 copy.118
  (99 shorter events, 19.0 us)
Async XLA Ops:
  9.6 1.3 %slice-start = ((bf16[590336]{0:T(1024)(128)(2,1)}), bf16[589824]{0:T(1024)(128)(2,1)S(1)}, s32[]{:S(2)}) async-start(bf16[590336]{0:T(1024)(128)(2,1)} %tile.9), calls=%async_computation.1 | async-start | bytes 2359296 | tf_op jit(solution)/shard_map/slice | solution.py:38
  12.2 1.4 %copy-start = (bf16[4608,1,128]{2,0,1:T(8,128)(2,1)S(1)}, bf16[4608,1,128]{2,0,1:T(8,128)(2,1)}, u32[]{:S(2)}) copy-start(bf16[4608,1,128]{2,0,1:T(8,128)(2,1)} %fusion) | copy-start | bytes 3538948
  61.0 2.6 %copy-start.1 = (bf16[4,4,2,5120]{3,2,1,0:T(2,128)(2,1)S(1)}, bf16[4,4,2,5120]{3,2,1,0:T(2,128)(2,1)}, u32[]{:S(2)}) copy-start(bf16[4,4,2,5120]{3,2,1,0:T(2,128)(2,1)} %param.6) | copy-start | bytes 983044
  65.7 8.4 %copy-start.9 = (bf16[4,4,2,64]{3,2,1,0:T(2,128)(2,1)S(1)}, bf16[4,4,2,64]{3,2,1,0:T(2,128)(2,1)}, u32[]{:S(2)}) copy-start(bf16[4,4,2,64]{3,2,1,0:T(2,128)(2,1)} %param.8) | copy-start | bytes 12292
  67.7 15.1 %all-to-all-start = ((bf16[32,2,128]{2,1,0:T(2,128)(2,1)}), bf16[32,2,128]{2,1,0:T(2,128)(2,1)S(1)}, u32[]{:S(2)}, u32[]{:S(2)}) async-start(bf16[32,2,128]{2,1,0:T(2,128)(2,1)} %reshape.168), calls=%async_computation | async-start | bytes 32768 | tf_op jit(solution)/shard_map/all_to_all | solution.py:137
  81.3 0.7 copy-start.10
  81.3 0.8 copy-start.11
  81.3 0.7 copy-start.12
  86.3 6.9 %collective-permute-start = (bf16[4,2,7,128]{3,2,1,0:T(8,128)(2,1)S(1)}, bf16[4,2,7,128]{3,2,1,0:T(8,128)(2,1)S(1)}, u32[]{:S(2)}, u32[]{:S(2)}) collective-permute-start(bf16[4,2,7,128]{3,2,1,0:T(8,128)(2,1)S(1)} %bitcast.138), channel_id=1, source_target_pairs={{1,0},{2,1},{3,2},{4,3},{5,4},{6,5},{7,6},{8,7},{9,8},{10,9},{11,1... | collective-permute-start | bytes 43016 | tf_op jit(solution)/shard_map/ppermute | solution.py:15
  93.5 2.2 %collective-permute-start.1 = (bf16[4,2,8,32]{3,2,1,0:T(8,128)(2,1)S(1)}, bf16[4,2,8,32]{3,2,1,0:T(8,128)(2,1)S(1)}, u32[]{:S(2)}, u32[]{:S(2)}) collective-permute-start(bf16[4,2,8,32]{3,2,1,0:T(8,128)(2,1)S(1)} %get-tuple-element.42), channel_id=1, source_target_pairs={} | collective-permute-start | bytes 12296 | tf_op jit(solution)/shard_map/ppermute | solution.py:26
  94.1 1.5 %collective-permute-start.2 = (bf16[4,2,8,32]{3,2,1,0:T(8,128)(2,1)S(1)}, bf16[4,2,8,32]{3,2,1,0:T(8,128)(2,1)S(1)}, u32[]{:S(2)}, u32[]{:S(2)}) collective-permute-start(bf16[4,2,8,32]{3,2,1,0:T(8,128)(2,1)S(1)} %get-tuple-element.43), channel_id=1, source_target_pairs={} | collective-permute-start | bytes 12296 | tf_op jit(solution)/shard_map/ppermute | solution.py:28
  99.0 6.9 %copy-start.2 = (bf16[4,2,8,32,1,4]{2,5,3,1,0,4:T(4,128)(2,1)S(1)}, bf16[4,2,8,32,1,4]{2,5,3,1,0,4:T(4,128)(2,1)}, u32[]{:S(2)}) copy-start(bf16[4,2,8,32,1,4]{2,5,3,1,0,4:T(4,128)(2,1)} %get-tuple-element.35) | copy-start | bytes 49156
  108.1 1.2 copy-start.6
  108.3 1.7 %copy-start.7 = (bf16[4,2,8,32,1,4]{3,2,5,4,1,0:T(8,128)(2,1)S(1)}, bf16[4,2,8,32,1,4]{3,2,5,4,1,0:T(8,128)(2,1)}, u32[]{:S(2)}) copy-start(bf16[4,2,8,32,1,4]{3,2,5,4,1,0:T(8,128)(2,1)} %copy.90) | copy-start | bytes 49156
  108.3 2.3 %copy-start.5 = (bf16[4,2,8,32,1,4]{3,2,5,4,1,0:T(8,128)(2,1)S(1)}, bf16[4,2,8,32,1,4]{3,2,5,4,1,0:T(8,128)(2,1)}, u32[]{:S(2)}) copy-start(bf16[4,2,8,32,1,4]{3,2,5,4,1,0:T(8,128)(2,1)} %copy.91) | copy-start | bytes 49156
  108.3 3.0 %copy-start.4 = (bf16[4,2,8,32,1,4]{3,2,5,4,1,0:T(8,128)(2,1)S(1)}, bf16[4,2,8,32,1,4]{3,2,5,4,1,0:T(8,128)(2,1)}, u32[]{:S(2)}) copy-start(bf16[4,2,8,32,1,4]{3,2,5,4,1,0:T(8,128)(2,1)} %copy.92) | copy-start | bytes 49156
  108.5 3.5 %copy-start.3 = (bf16[4,2,8,32,1,4]{3,2,5,4,1,0:T(8,128)(2,1)S(1)}, bf16[4,2,8,32,1,4]{3,2,5,4,1,0:T(8,128)(2,1)}, u32[]{:S(2)}) copy-start(bf16[4,2,8,32,1,4]{3,2,5,4,1,0:T(8,128)(2,1)} %copy.93) | copy-start | bytes 49156
  109.4 10.4 %copy-start.8 = (bf16[4,2,4,544,1]{3,2,1,0,4:T(4,128)(2,1)S(1)}, bf16[4,2,4,544,1]{3,2,1,0,4:T(4,128)(2,1)}, u32[]{:S(2)}) copy-start(bf16[4,2,4,544,1]{3,2,1,0,4:T(4,128)(2,1)} %reshape.164) | copy-start | bytes 104452
where the time goes:
time: 123 us; the launch traced here: 122 us
  local copies, waits for them, and re-layouts  99.6 us (81%)
  starting transfers between devices  9.96 us (8%)
  other arithmetic  4.9 us (4%)
  waiting for transfers between devices  4.52 us (4%)
  matrix products  2.73 us (2%)
    another operation x1, local copies, waits for them, and re-layouts, range_matrix(): matrix = jnp.stack([from_real, from_imag], 0)  44.9 us
    unnamed x47, local copies, waits for them, and re-layouts  16.3 us
    another operation x19, local copies, waits for them, and re-layouts, azimuth(): jnp.stack([quartets[:, :, :, shift_step:shift_step + pulses // 4, :] for...  13.2 us
    gather x2, local copies, waits for them, and re-layouts, azimuth(): picked = jnp.where(inside, jnp.take(filters, tap_index, axis=3), 0)  6.52 us
    all_to_all x1, starting transfers between devices, body(): lax.all_to_all(compressed, 'pulse', split_axis=2, concat_axis=3, tiled=True)  6.39 us
    another operation x4, local copies, waits for them, and re-layouts, banded(): tiled = jnp.tile(extended, block_len)[:block_len * span_len]  5.35 us
    ppermute x1, waiting for transfers between devices, passed_along(): return lax.ppermute(array, axis, pairs)  4.52 us
    reshape x3, local copies, waits for them, and re-layouts, banded(): return tiled.reshape(block_len, span_len).T  3.4 us
  transfers between devices with their start and end apart: 4, of which 1 were waited for; matrix products, arithmetic and copies ran while one was open for 7% of the time, Pallas kernels for 0%

commit v1 on v0

v1 whole, which is shorter than its diff:
```python
import functools

import jax
import jax.numpy as jnp
from jax import lax
from jax.experimental import pallas as pl
from jax.experimental.pallas import tpu as pltpu
from jax.sharding import PartitionSpec as P

LANES = 128
STEP = 4
BLOCK = LANES // STEP
NT = (((1,), (1,)), ((), ()))


def dot_nt(a, b):
    return lax.dot_general(a, b, NT, preferred_element_type=jnp.float32)


def range_rows(replica_ref, bmat_ref, bins, depth):
    span = 2 * bins
    windows = BLOCK // bins
    rows = BLOCK + bins
    taps = replica_ref.shape[1]
    replica = replica_ref[...].astype(jnp.float32)
    shifted = []
    for part in range(2):
        row = jnp.concatenate([replica[part : part + 1], jnp.zeros((1, depth - taps), jnp.float32)], axis=1)
        shifted.append(
            pltpu.roll(jnp.broadcast_to(row, (rows, depth)), 0, 1, stride=STEP, stride_axis=0)
        )
    real, imag = shifted
    half = windows * 2 * span
    for window in range(windows):
        low = window * bins
        real_part = real[low : low + span].astype(jnp.bfloat16)
        imag_part = imag[low : low + span].astype(jnp.bfloat16)
        at = window * 2 * span
        bmat_ref[at : at + span, :] = real_part
        bmat_ref[at + span : at + 2 * span, :] = imag_part
        bmat_ref[half + at : half + at + span, :] = -imag_part
        bmat_ref[half + at + span : half + at + 2 * span, :] = real_part


def azimuth_rows(filters_ref, tt_ref, step):
    samples, channels, _, taps = filters_ref.shape
    for s in range(samples):
        for c in range(channels):
            taps_row = filters_ref[s, c].astype(jnp.float32)
            taps_row = jnp.concatenate([taps_row, jnp.zeros((2, LANES - taps), jnp.float32)], axis=1)
            real, imag = [
                pltpu.roll(
                    jnp.broadcast_to(taps_row[part : part + 1], (step, LANES)), 0, 1, stride=1, stride_axis=0
                ).astype(jnp.bfloat16)
                for part in range(2)
            ]
            top, left = s * 2 * step, c * 2 * LANES
            tt_ref[top : top + step, left : left + LANES] = real
            tt_ref[top + step : top + 2 * step, left : left + LANES] = imag
            tt_ref[top : top + step, left + LANES : left + 2 * LANES] = -imag
            tt_ref[top + step : top + 2 * step, left + LANES : left + 2 * LANES] = real


def column(values, count):
    ids = lax.broadcasted_iota(jnp.int32, (count, LANES), 0)
    total = jnp.zeros((count, LANES), jnp.int32)
    for r in range(count):
        total = jnp.where(ids == r, values(r), total)
    return total


def kernel(
    n, whole_image,
    echoes_ref, replica_ref, filters_ref, offset_ref, width_ref, edges_ref,
    out_ref,
    raw, lines, bmat, tt, product, send, recv, turned,
    in_sem, send_sem, recv_sem,
):
    me = lax.axis_index("pulse")
    channels, pulses, _, samples = echoes_ref.shape
    taps = replica_ref.shape[1]
    depth = bmat.shape[1]
    bin_count = (samples - taps) // STEP
    bins = bin_count // n
    span = 2 * bins
    windows = BLOCK // bins
    piece = 2 * span
    pairs = channels * pulses

    fetch = pltpu.make_async_copy(echoes_ref, raw, in_sem)
    fetch.start()

    barrier = pltpu.get_barrier_semaphore()

    @pl.loop(1, n)
    def _(k):
        pl.semaphore_signal(
            barrier, inc=1, device_id={"pulse": lax.rem(me + k, n)}, device_id_type=pl.DeviceIdType.MESH
        )

    range_rows(replica_ref, bmat, bins, depth)
    fetch.wait()
    for c in range(channels):
        for p in range(pulses):
            at = 2 * (c * pulses + p)
            lines[at : at + 2, :samples] = raw[c, p]
    lines[:, samples:] = jnp.zeros((2 * pairs, lines.shape[1] - samples), lines.dtype)

    blocks = bin_count // BLOCK
    group = min(blocks, 8)
    rows = 2 * pulses
    lane = lax.broadcasted_iota(jnp.int32, (group * pulses, LANES), 1)
    for first in range(0, blocks, group):
        rows_in = jnp.concatenate(
            [lines[:, LANES * a : LANES * a + depth] for a in range(first, first + group)], axis=0
        )
        result = dot_nt(rows_in, bmat[...])
        for a in range(group):
            for c in range(channels):
                at = (a * channels + c) * rows
                for half in range(2):
                    product[half, c, a * rows : (a + 1) * rows, :] = result[
                        at : at + rows, half * LANES : (half + 1) * LANES
                    ]
        by_channel = [
            product[0, c, pl.ds(0, group * pulses, stride=2), :]
            + product[1, c, pl.ds(1, group * pulses, stride=2), :]
            for c in range(channels)
        ]
        for w in range(windows):
            message = None
            for c in range(channels):
                shift = (piece * (c - w)) % LANES
                moved = pltpu.roll(by_channel[c], shift, 1) if shift else by_channel[c]
                message = moved if c == 0 else jnp.where(lane >= piece * c, moved, message)
            for a in range(group):
                send[(first + a) * windows + w] = message[a * pulses : (a + 1) * pulses].astype(send.dtype)

    pl.semaphore_wait(barrier, n - 1)

    @pl.loop(1, n)
    def _(k):
        to = lax.rem(me + k, n)
        pltpu.make_async_remote_copy(
            src_ref=send.at[to], dst_ref=recv.at[me], send_sem=send_sem, recv_sem=recv_sem,
            device_id={"pulse": to}, device_id_type=pl.DeviceIdType.MESH,
        ).start()

    recv[me] = send[me]

    all_pulses = n * pulses
    row_id = lax.broadcasted_iota(jnp.int32, (bins, LANES), 0)
    lane_id = lax.broadcasted_iota(jnp.int32, (bins, LANES), 1)
    first_bin = row_id + column(lambda r: offset_ref[r], bins)
    width = column(lambda r: width_ref[r], bins)
    low_edge = column(lambda r: edges_ref[0, r], bins)
    high_edge = all_pulses - column(lambda r: edges_ref[1, r], bins)
    place = lane_id % span
    chosen = (place >= first_bin) & (place < first_bin + width) & (place + me * bins < bin_count)
    select = jnp.concatenate(
        [
            jnp.where(chosen & (lane_id // span == g), 1.0, 0.0)
            for g in range(2 * channels)
        ],
        axis=0,
    ).astype(jnp.bfloat16)
    scale = 1.0 / width.astype(jnp.float32)

    margin = (turned.shape[0] - all_pulses) // 2
    if whole_image:
        turned[0:margin, :] = jnp.zeros((margin, LANES), jnp.float32)
        turned[margin + all_pulses :, :] = jnp.zeros((margin, LANES), jnp.float32)
        azimuth_rows(filters_ref, tt, tt.shape[0] // (2 * filters_ref.shape[0]))

    pltpu.make_async_copy(send.at[pl.ds(0, n - 1)], recv.at[pl.ds(0, n - 1)], recv_sem).wait()

    for i in range(n):
        turned[margin + i * pulses : margin + (i + 1) * pulses, :] = recv[i].astype(jnp.float32)

    def corrected(start):
        taken = dot_nt(select, turned[start : start + LANES, :].astype(jnp.bfloat16))
        pulse = lane_id + (start - margin)
        weight = jnp.where((pulse >= low_edge) & (pulse < high_edge), scale, 0.0)
        return [taken[g * bins : (g + 1) * bins] * weight for g in range(2 * channels)]

    if whole_image:
        samples_out = filters_ref.shape[0]
        step = LANES // 2
        rows_in = jnp.concatenate(
            [jnp.concatenate(corrected(start), axis=1) for start in range(0, all_pulses, step)], axis=0
        ).astype(jnp.bfloat16)
        image = dot_nt(rows_in, tt[...])
        left = lane_id < step
        for s in range(samples_out):
            for b in range(all_pulses // LANES):
                at = 2 * b * bins
                early = image[at : at + bins, s * LANES : (s + 1) * LANES]
                late = image[at + bins : at + 2 * bins, s * LANES : (s + 1) * LANES]
                real = jnp.where(left, early, pltpu.roll(late, step, 1))
                imag = jnp.where(left, pltpu.roll(early, step, 1), late)
                out_ref[s, 0, :, b * LANES : (b + 1) * LANES] = real.astype(out_ref.dtype)
                out_ref[s, 1, :, b * LANES : (b + 1) * LANES] = imag.astype(out_ref.dtype)
    else:
        for b in range(all_pulses // LANES):
            for g, part in enumerate(corrected(b * LANES)):
                out_ref[g // 2, g % 2, :, b * LANES : (b + 1) * LANES] = part.astype(out_ref.dtype)

    pltpu.make_async_copy(send.at[pl.ds(0, n - 1)], recv.at[pl.ds(0, n - 1)], send_sem).wait()


def run_kernel(echoes, replica, recon_filters, span_offset, span_width, aperture_edges, whole_image):
    n = lax.axis_size("pulse")
    channels, pulses, _, samples = echoes.shape
    taps = replica.shape[1]
    bin_count = (samples - taps) // STEP
    bins = bin_count // n
    span = 2 * bins
    all_pulses = n * pulses
    blocks = bin_count // BLOCK
    group = min(blocks, 8)
    assert BLOCK % bins == 0 and channels * 2 * span == LANES and channels == BLOCK // bins
    assert blocks % group == 0 and all_pulses % LANES == 0
    depth = taps + 2 * LANES
    samples_out, _, _, az_taps = recon_filters.shape
    step = LANES // 2
    assert az_taps == step
    if whole_image:
        margin = az_taps // 2
        out_shape = (samples_out, 2, bins, all_pulses)
        tt_shape = (samples_out * 2 * step, channels * 2 * LANES)
    else:
        margin = 0
        out_shape = (channels, 2, bins, all_pulses)
        tt_shape = (16, LANES)
    vmem = pl.BlockSpec(memory_space=pltpu.VMEM)
    smem = pl.BlockSpec(memory_space=pltpu.SMEM)
    return pl.pallas_call(
        functools.partial(kernel, n, whole_image),
        out_shape=jax.ShapeDtypeStruct(out_shape, jnp.bfloat16),
        in_specs=[pl.BlockSpec(memory_space=pl.ANY), vmem, vmem, smem, smem, smem],
        out_specs=vmem,
        scratch_shapes=[
            pltpu.VMEM(echoes.shape, jnp.bfloat16),
            pltpu.VMEM((2 * channels * pulses, samples + LANES), jnp.bfloat16),
            pltpu.VMEM((2 * LANES, depth), jnp.bfloat16),
            pltpu.VMEM(tt_shape, jnp.bfloat16),
            pltpu.VMEM((2, channels, group * 2 * pulses, LANES), jnp.float32),
            pltpu.VMEM((n, pulses, LANES), jnp.bfloat16),
            pltpu.VMEM((n, pulses, LANES), jnp.bfloat16),
            pltpu.VMEM((all_pulses + 2 * margin, LANES), jnp.float32),
            pltpu.SemaphoreType.DMA,
            pltpu.SemaphoreType.DMA,
            pltpu.SemaphoreType.DMA,
        ],
        compiler_params=pltpu.CompilerParams(
            collective_id=0, has_side_effects=True, vmem_limit_bytes=48 * 1024 * 1024
        ),
    )(echoes, replica, recon_filters, span_offset, span_width, aperture_edges)


def with_neighbours(cells, axis, dim, width):
    count = lax.axis_size(axis)
    head = lax.slice_in_dim(cells, 0, width, axis=dim)
    tail = lax.slice_in_dim(cells, cells.shape[dim] - width, cells.shape[dim], axis=dim)
    up = [(i, i + 1) for i in range(count - 1)]
    down = [(i + 1, i) for i in range(count - 1)]
    return jnp.concatenate(
        [lax.ppermute(tail, axis, up), cells, lax.ppermute(head, axis, down)], axis=dim
    )


def azimuth(padded, filters):
    channels, _, bin_count, padded_len = padded.shape
    subbands = filters.shape[0]
    tap_count = filters.shape[3]
    pulses = padded_len - tap_count
    span_len = tap_count + 4
    step_count = span_len // 4
    quartets = padded.reshape(channels, 2, bin_count, padded_len // 4, 4)
    window = jnp.stack(
        [quartets[:, :, :, first : first + pulses // 4, :] for first in range(step_count)], 4
    )
    window = window.transpose(2, 3, 0, 1, 4, 5).reshape(
        bin_count * (pulses // 4), channels * 2 * span_len
    )
    offset = jnp.arange(span_len)[:, None] - jnp.arange(4)[None, :]
    inside = (offset >= 0) & (offset < tap_count)
    picked = jnp.where(inside, jnp.take(filters, jnp.clip(offset, 0, tap_count - 1), axis=3), 0)
    real, imag = picked[:, :, 0], picked[:, :, 1]
    matrix = jnp.stack([jnp.stack([real, imag], 3), jnp.stack([-imag, real], 3)], 2)
    matrix = matrix.transpose(1, 2, 3, 0, 4, 5).reshape(channels * 2 * span_len, subbands * 8)
    result = jnp.dot(window, matrix, preferred_element_type=jnp.float32)
    result = result.reshape(bin_count, pulses // 4, subbands, 2, 4).transpose(2, 3, 0, 1, 4)
    return result.reshape(subbands, 2, bin_count, pulses)


def body(echoes, replica, recon_filters, span_offset, span_width, aperture_edges):
    operands = (echoes, replica, recon_filters, span_offset, span_width, aperture_edges)
    if lax.axis_size("chan") == 1 and echoes.shape[0] == recon_filters.shape[1]:
        return run_kernel(*operands, whole_image=True)
    corrected = run_kernel(*operands, whole_image=False)
    corrected = lax.all_to_all(corrected, "chan", split_axis=3, concat_axis=0, tiled=True)
    padded = with_neighbours(corrected, "chan", 3, recon_filters.shape[3] // 2)
    return azimuth(padded, recon_filters).astype(jnp.bfloat16)


def solution(mesh):
    return jax.shard_map(
        body,
        mesh=mesh,
        in_specs=(
            P("chan", "pulse", None, None),
            P(),
            P(),
            P("pulse"),
            P("pulse"),
            P(None, "pulse"),
        ),
        out_specs=P(None, None, "pulse", "chan"),
        check_vma=False,
    )
```

time: 123 us -> 17.1 us (0.14)
  the two profiles are of different devices: /device:TPU:7 before, /device:TPU:0 now
where the time goes in v1:
time: 17.1 us; the launch traced here: 16.8 us
  Pallas kernels  11.8 us (69%)
  local copies, waits for them, and re-layouts  4.98 us (29%)
    pallas_call x1, Pallas kernels, run_kernel(): pl.pallas_call(functools.partial(kernel, n, whole_image), out_shape=jax.S...  11.8 us
    unnamed x13, local copies, waits for them, and re-layouts  4.98 us

profile of v1, /device:TPU:0, one launch (start us, length us, event | category | flops | bytes accessed | tf_op | source)
XLA Modules:
  0.0 16.8 jit_solution(3757637337443648481)
XLA Ops:
  0.0 0.0 copy-start
  0.0 1.0 %copy-done = bf16[4,4,2,5120]{3,2,1,0:T(2,128)(2,1)S(1)} copy-done((bf16[4,4,2,5120]{3,2,1,0:T(2,128)(2,1)S(1)}, bf16[4,4,2,5120]{3,2,1,0:T(2,128)(2,1)}, u32[]{:S(2)}) %copy-start) | copy-done | bytes 327704
  1.0 0.0 copy-start.1
  1.0 0.7 %copy-done.1 = bf16[2,4096]{1,0:T(2,128)(2,1)S(1)} copy-done((bf16[2,4096]{1,0:T(2,128)(2,1)S(1)}, bf16[2,4096]{1,0:T(2,128)(2,1)}, u32[]{:S(2)}) %copy-start.1) | copy-done | bytes 16408
  1.7 0.0 copy-start.2
  1.7 0.7 %copy-done.2 = bf16[4,4,2,64]{3,2,1,0:T(2,128)(2,1)S(1)} copy-done((bf16[4,4,2,64]{3,2,1,0:T(2,128)(2,1)S(1)}, bf16[4,4,2,64]{3,2,1,0:T(2,128)(2,1)}, u32[]{:S(2)}) %copy-start.2) | copy-done | bytes 4120
  2.4 0.0 copy-start.3
  2.4 0.7 %copy-done.3 = s32[2,8]{1,0:T(2,128)S(1)} copy-done((s32[2,8]{1,0:T(2,128)S(1)}, s32[2,8]{1,0:T(2,128)}, u32[]{:S(2)}) %copy-start.3) | copy-done | bytes 88
  3.1 0.0 copy-start.4
  3.1 0.7 %copy-done.4 = s32[8]{0:T(128)S(1)} copy-done((s32[8]{0:T(128)S(1)}, s32[8]{0:T(128)}, u32[]{:S(2)}) %copy-start.4) | copy-done | bytes 56
  3.7 0.0 copy-start.5
  3.7 0.7 %copy-done.5 = s32[8]{0:T(128)S(1)} copy-done((s32[8]{0:T(128)S(1)}, s32[8]{0:T(128)}, u32[]{:S(2)}) %copy-start.5) | copy-done | bytes 56
  4.4 11.8 %shard_map.64 = bf16[4,2,8,128]{3,2,1,0:T(8,128)(2,1)S(1)} custom-call(bf16[4,4,2,5120]{3,2,1,0:T(2,128)(2,1)S(1)} %copy-done, bf16[2,4096]{1,0:T(2,128)(2,1)S(1)} %copy-done.1, bf16[4,4,2,64]{3,2,1,0:T(2,128)(2,1)S(1)} %copy-done.2, s32[8]{0:T(128)S(1)} %copy-done.4, s32[8]{0:T(128)S(1)} %copy-done.5, s32[2,8]{1,0:T(2,128)S(1)} %copy-done.3), custom_call_target="tpu_custom_call" | custom-call | tf_op jit(solution)/shard_map/pallas_call | solution.py:237
  16.2 0.6 %copy.8 = bf16[4,2,8,128]{3,2,1,0:T(8,128)(2,1)} copy(bf16[4,2,8,128]{3,2,1,0:T(8,128)(2,1)S(1)} %shard_map.64) | data formatting | bytes 32768
Async XLA Ops:
  0.0 1.0 %copy-start = (bf16[4,4,2,5120]{3,2,1,0:T(2,128)(2,1)S(1)}, bf16[4,4,2,5120]{3,2,1,0:T(2,128)(2,1)}, u32[]{:S(2)}) copy-start(bf16[4,4,2,5120]{3,2,1,0:T(2,128)(2,1)} %echoes_ref.1) | copy-start | bytes 983044
  1.0 0.7 %copy-start.1 = (bf16[2,4096]{1,0:T(2,128)(2,1)S(1)}, bf16[2,4096]{1,0:T(2,128)(2,1)}, u32[]{:S(2)}) copy-start(bf16[2,4096]{1,0:T(2,128)(2,1)} %replica_ref.1) | copy-start | bytes 49156
  1.7 0.7 %copy-start.2 = (bf16[4,4,2,64]{3,2,1,0:T(2,128)(2,1)S(1)}, bf16[4,4,2,64]{3,2,1,0:T(2,128)(2,1)}, u32[]{:S(2)}) copy-start(bf16[4,4,2,64]{3,2,1,0:T(2,128)(2,1)} %filters_ref.1) | copy-start | bytes 12292
  2.4 0.7 %copy-start.3 = (s32[2,8]{1,0:T(2,128)S(1)}, s32[2,8]{1,0:T(2,128)}, u32[]{:S(2)}) copy-start(s32[2,8]{1,0:T(2,128)} %edges_ref.1) | copy-start | bytes 196
  3.1 0.7 %copy-start.4 = (s32[8]{0:T(128)S(1)}, s32[8]{0:T(128)}, u32[]{:S(2)}) copy-start(s32[8]{0:T(128)} %offset_ref.1) | copy-start | bytes 100
  3.7 0.7 %copy-start.5 = (s32[8]{0:T(128)S(1)}, s32[8]{0:T(128)}, u32[]{:S(2)}) copy-start(s32[8]{0:T(128)} %width_ref.1) | copy-start | bytes 100
